TPU v7x, 32 devices: a whole 2x2x4 slice. The times are simulated.
32 devices in a mesh: groups: 2 (over y), expert: 8 (over z, x), head: 2 (over core).
Axes of the slice: x: 2, y: 2, z: 4, core: 2. Of those that a mesh axis runs over, the one named last changes fastest.
Arguments:
- stream: bfloat16 [2, 16, 4096], P(None, ('groups', 'expert')), parts along dimension 1, may hold values from -6 to 6
- heads_in: bfloat16 [2, 16, 8192], P(None, ('groups', 'expert'), 'head'), parts along dimension 1, may hold values from -6 to 6
- heads_gate: bfloat16 [2, 16, 8192], P(None, ('groups', 'expert'), 'head'), parts along dimension 1, may hold values from -6 to 6
- write_key: bfloat16 [2, 16, 64], P(None, ('groups', 'expert')), parts along dimension 1, may hold values from -6 to 6
- read_query: bfloat16 [2, 16, 64], P(None, ('groups', 'expert')), parts along dimension 1, may hold values from -0.75 to 0.75
- step_size: float32 [2, 16, 128], P(None, ('groups', 'expert'), 'head'), parts along dimension 1, may hold values from 0.05 to 1
- state_cache: bfloat16 [16, 128, 4096], P(('groups', 'expert'), 'head'), parts along dimension 0, may hold values from -6 to 6
- decay_rate: float32 [128], P('head'), may hold values from 0.5 to 8
- skip_gain: float32 [128], P('head'), may hold values from 0.5 to 1.5
- out_weight: bfloat16 [8192, 4096], P('head', 'expert'), may hold values from -0.0625 to 0.0625
- norm_gain: float32 [4096], replicated, may hold values from 0.5 to 1.5
- up_weight: bfloat16 [4096, 65536], P(None, ('expert', 'head')), may hold values from -0.09375 to 0.09375
- down_weight: bfloat16 [65536, 4096], P(('expert', 'head')), may hold values from -0.046875 to 0.046875
- expert_ids: int32 [2, 16, 2], P(None, ('groups', 'expert')), parts along dimension 1, may hold values from 0 to 3, all different within a row
- expert_gates: bfloat16 [2, 16, 2], P(None, ('groups', 'expert')), parts along dimension 1, may hold values from 0.19921875 to 1
Outputs:
- layer_out: bfloat16 [2, 16, 4096], P(None, ('groups', 'expert')), parts along dimension 1
There are 2 independent parts, one for each index of `groups`. A program takes and returns all parts, laid end to end along the dimension named above; an argument that names none is the same for every part. Nothing has to cross between parts.
Inputs may be any that keep to these rules, and one draw needn't show every extreme that they name: `expert_ids`: each token names 2 different experts.
All inputs are finite; a program needn't handle non-finite values.
Results may differ from a plain program's by a relative error of at most 0.0056.
Values may be sent and summed in bfloat16 or wider, within the bound.
A program may use at most 192 MiB of HBM per device.

v0:
```python
import jax
import jax.numpy as jnp
from jax import lax
from jax.sharding import PartitionSpec as P

P_SIZE = 64
N = 64
EXPERTS = 4
FF = 16384
STEPS = 2


EPSILON = 1e-05


def finish(
    mixer, stream, expert_ids, expert_gates, out_weight, norm_gain, up_weight, down_weight, owner
):
    partial_out = jnp.einsum(
        "srk,kc->src",
        lax.all_gather(mixer, "expert", axis=1, tiled=True),
        out_weight,
        preferred_element_type=jnp.float32,
    )
    summed = lax.psum(partial_out, "head")
    mixed = lax.all_to_all(summed, "expert", split_axis=1, concat_axis=2, tiled=True)
    middle = (stream.astype(jnp.float32) + mixed).astype(jnp.bfloat16)
    wide = middle.astype(jnp.float32)
    scale = lax.rsqrt(jnp.mean(wide * wide, axis=-1, keepdims=True) + EPSILON)
    normed = (wide * scale * norm_gain[None, None, :]).astype(jnp.bfloat16)
    experts = lax.broadcasted_iota(jnp.int32, (1, 1, 1, EXPERTS), 3)
    table = jnp.sum(
        jnp.where(
            expert_ids[:, :, :, None] == experts,
            expert_gates[:, :, :, None].astype(jnp.float32),
            jnp.float32(0.0),
        ),
        axis=2,
    ).astype(jnp.bfloat16)
    every_token, every_table = (
        lax.all_gather(normed, "expert", axis=1, tiled=True),
        lax.all_gather(table, "expert", axis=1, tiled=True),
    )
    picker = lax.broadcasted_iota(jnp.int32, (1, 1, EXPERTS), 2) == owner
    weight_row = jnp.sum(
        jnp.where(picker, every_table.astype(jnp.float32), jnp.float32(0.0)), axis=2
    )
    lifted = jnp.einsum("std,dc->tsc", every_token, up_weight, preferred_element_type=jnp.float32)
    hidden = (jax.nn.gelu(lifted) * jnp.transpose(weight_row)[:, :, None]).astype(jnp.bfloat16)
    combined = lax.psum_scatter(
        jnp.einsum("tsc,cd->tsd", hidden, down_weight, preferred_element_type=jnp.float32),
        "expert",
        scatter_dimension=0,
        tiled=True,
    )
    total = lax.psum(combined, "head")
    return (wide + jnp.transpose(total, (1, 0, 2))).astype(jnp.bfloat16)


def on_device(
    stream,
    heads_in,
    heads_gate,
    write_key,
    read_query,
    step_size,
    state_cache,
    decay_rate,
    skip_gain,
    out_weight,
    norm_gain,
    up_weight,
    down_weight,
    expert_ids,
    expert_gates,
):
    local_rows = heads_in.shape[1]
    local_width = heads_in.shape[2]
    local_heads = decay_rate.shape[0]
    state = state_cache.astype(jnp.float32).reshape(local_rows, local_heads, P_SIZE, N)
    position = lax.axis_index("expert") * lax.axis_size("head") + lax.axis_index("head")
    owner = position * up_weight.shape[1] // FF
    mixers = []
    for step in range(STEPS):
        values = heads_in[step].astype(jnp.float32).reshape(local_rows, local_heads, P_SIZE)
        delta = step_size[step]
        keys = write_key[step].astype(jnp.float32)
        query = read_query[step].astype(jnp.float32)
        factor = jnp.exp(-delta * decay_rate[None, :])
        state = (
            factor[:, :, None, None] * state
            + (delta[:, :, None] * values)[:, :, :, None] * keys[:, None, None, :]
        )
        read = (
            jnp.einsum("thpn,tn->thp", state, query, precision=lax.Precision.HIGHEST)
            + skip_gain[None, :, None] * values
        )
        gate = heads_gate[step].astype(jnp.float32).reshape(local_rows, local_heads, P_SIZE)
        mixers.append((read * jax.nn.silu(gate)).reshape(local_rows, local_width).astype(jnp.bfloat16))
    return finish(
        jnp.stack(mixers),
        stream,
        expert_ids,
        expert_gates,
        out_weight,
        norm_gain,
        up_weight,
        down_weight,
        owner,
    )


def solution(mesh):
    placed = (
        P(None, ("groups", "expert"), None),
        P(None, ("groups", "expert"), "head"),
        P(None, ("groups", "expert"), "head"),
        P(None, ("groups", "expert"), None),
        P(None, ("groups", "expert"), None),
        P(None, ("groups", "expert"), "head"),
        P(("groups", "expert"), "head", None),
        P("head"),
        P("head"),
        P("head", "expert"),
        P(),
        P(None, ("expert", "head")),
        P(("expert", "head"), None),
        P(None, ("groups", "expert"), None),
        P(None, ("groups", "expert"), None),
    )
    return jax.shard_map(
        on_device,
        mesh=mesh,
        in_specs=placed,
        out_specs=P(None, ("groups", "expert"), None),
        check_vma=False,
    )
```

profile of v0, /device:TPU:0, one launch (start us, length us, event | category | flops | bytes accessed | tf_op | source)
XLA Modules:
  0.0 229.8 jit_solution(18445587839326030084)
XLA Ops:
  6.5 1.0 convert_reduce_fusion.2
  7.6 0.7 slice_bitcast_fusion.1
  8.3 0.6 mul.216
  9.0 0.7 mul.217
  9.8 0.6 mul.231
  10.4 1.6 mul.232
  12.2 3.0 %multiply_add_fusion = (f32[1,64,4096]{2,1,0:T(8,128)}, f32[1,64,4096]{2,1,0:T(8,128)}) fusion(f32[1,64,4096]{2,1,0:T(8,128)} %mul.232, f32[4096]{0:T(1024)S(1)} %mul.234, f32[64]{0:T(128)S(1)} %get-tuple-element.14, f32[1,64,4096]{2,1,0:T(8,128)S(1)} %mul.217, f32[4096]{0:T(1024)S(1)} %mul.219, bf16[1,64,4096]{2,1,0:T(8,128)(2,1)} %param.21, ...), kind=kLoop, calls=%fused_computation.7 | loop fusion | flops 1835008 | bytes 4751872 | tf_op jit(solution)/shard_map/add | solution.py:91
  15.2 2.0 add.76
  17.3 3.1 %add.72 = f32[64,64,64]{2,1,0:T(8,128)} reshape(f32[1,64,4096]{2,1,0:T(8,128)} %get-tuple-element.12) | data formatting | bytes 2097152 | tf_op jit(solution)/shard_map/add | solution.py:91
  20.4 2.5 %fusion.35 = f32[1,64,64]{2,0,1:T(1,128)S(1)} fusion(f32[64,64,64]{2,1,0:T(8,128)S(1)} %add.76, bf16[2,1,64]{2,0,1:T(2,128)(2,1)S(1)} %copy-done.3), kind=kOutput, calls=%fused_computation.43 | convolution fusion | flops 3145728 | bytes 1065216 | tf_op jit(solution)/shard_map/thpn,tn->thp/dot_general | solution.py:95
  23.0 4.2 %fusion.37 = f32[1,64,64]{2,0,1:T(1,128)S(1)} fusion(f32[64,64,64]{2,1,0:T(8,128)} %add.72, bf16[2,1,64]{2,0,1:T(2,128)(2,1)S(1)} %copy-done.3), kind=kOutput, calls=%fused_computation.46 | convolution fusion | flops 3145728 | bytes 1065216 | tf_op jit(solution)/shard_map/thpn,tn->thp/dot_general | solution.py:95
  27.6 32.3 %all_gather.9 = bf16[2,8,4096]{2,0,1:T(2,128)(2,1)S(1)} all-gather(bf16[2,1,4096]{2,0,1:T(2,128)(2,1)S(1)} %pad_maximum_fusion), channel_id=1, replica_groups=mesh['groups'=2,'expert'=8,'head'=2] {'expert'}, dimensions={1}, use_global_device_ids=true | all-gather | bytes 147456 | tf_op jit(solution)/shard_map/all_gather | solution.py:21
  59.9 2.8 %fusion.7 = f32[2,8,512]{2,1,0:T(8,128)S(1)} fusion(bf16[4096,512]{1,0:T(8,128)(2,1)} %param.24, bf16[2,8,4096]{2,0,1:T(2,128)(2,1)S(1)} %all_gather.9), kind=kOutput, calls=%fused_computation.5 | convolution fusion | flops 67108864 | bytes 4358144 | tf_op jit(solution)/shard_map/srk,kc->src/dot_general | solution.py:19
  62.8 3.4 %psum.14 = f32[2,8,512]{2,1,0:T(8,128)S(1)} all-reduce(f32[2,8,512]{2,1,0:T(8,128)S(1)} %fusion.7), channel_id=1, replica_groups=mesh['groups'=2,'expert'=8,'head'=2] {'head'}, use_global_device_ids=true, to_apply=%region_0.1 | all-reduce | flops 8192 | bytes 65536 | tf_op jit(solution)/shard_map/psum | solution.py:25
  66.2 0.6 copy.35
  66.8 5.5 %all-to-all-start = ((f32[2,8,512]{2,0,1:T(2,128)}), f32[2,8,512]{2,0,1:T(2,128)S(1)}, u32[]{:S(2)}, u32[]{:S(2)}) async-start(f32[2,8,512]{2,0,1:T(2,128)} %copy.35), calls=%async_computation | async-start | bytes 65536 | tf_op jit(solution)/shard_map/all_to_all | solution.py:26
  72.5 20.8 %all-gather.1 = bf16[8,4,2]{1,2,0:T(2,128)(2,1)S(1)} all-gather(bf16[1,4,2]{1,2,0:T(2,128)(2,1)S(1)} %bitcast.81), channel_id=2, replica_groups=mesh['groups'=2,'expert'=8,'head'=2] {'expert'}, dimensions={0}, use_global_device_ids=true | all-gather | bytes 144 | tf_op jit(solution)/shard_map/all_gather | solution.py:42
  94.0 30.7 %all_gather.10 = bf16[2,8,4096]{2,0,1:T(2,128)(2,1)S(1)} all-gather(bf16[2,1,4096]{2,0,1:T(2,128)(2,1)S(1)} %fusion.28), channel_id=1, replica_groups=mesh['groups'=2,'expert'=8,'head'=2] {'expert'}, dimensions={1}, use_global_device_ids=true | all-gather | bytes 147456 | tf_op jit(solution)/shard_map/all_gather | solution.py:41
  124.7 23.8 %fusion = f32[8,2,4096]{2,0,1:T(8,128)S(1)} fusion(bf16[4096,4096]{1,0:T(8,128)(2,1)} %param.27, bf16[4096,4096]{1,0:T(8,128)(2,1)} %param.26, bf16[2,8,4096]{2,0,1:T(2,128)(2,1)S(1)} %all_gather.10, f32[8,2]{0,1:T(2,128)S(1)} %bitcast.79), kind=kOutput, calls=%fused_computation | convolution fusion | flops 1074397184 | bytes 67502144 | tf_op jit(solution)/shard_map/tsc,cd->tsd/dot_general | solution.py:51
  148.5 0.9 copy.39
  150.1 67.4 %all-reduce.3.cloned.1.call-done = f32[8,2,4096]{2,1,0:T(2,128)} async-done(((f32[8,2,4096]{2,1,0:T(2,128)}), f32[8,2,4096]{2,1,0:T(2,128)}) %all-reduce.3.cloned.1.call-update) | async-done | bytes 262160
  217.5 1.4 dynamic-slice_bitcast_fusion
  218.9 3.4 %psum.15 = f32[2,1,4096]{2,0,1:T(2,128)S(1)} all-reduce(f32[2,1,4096]{2,0,1:T(2,128)S(1)} %dynamic-slice_bitcast_fusion), channel_id=1, replica_groups=mesh['groups'=2,'expert'=8,'head'=2] {'head'}, use_global_device_ids=true, to_apply=%region_5.6 | all-reduce | flops 8192 | bytes 65536 | tf_op jit(solution)/shard_map/psum | solution.py:56
  222.3 0.6 fusion.29
  (51 shorter events, 2.4 us)
Async XLA Ops:
  8.9 3.1 %copy-start.4 = (bf16[2,1,64]{2,0,1:T(2,128)(2,1)S(1)}, bf16[2,1,64]{2,0,1:T(2,128)(2,1)}, u32[]{:S(2)}) copy-start(bf16[2,1,64]{2,0,1:T(2,128)(2,1)} %param.18) | copy-start | bytes 772
  9.0 3.3 %copy-start.2 = (f32[2,1,64]{2,1,0:T(1,128)S(1)}, f32[2,1,64]{2,1,0:T(1,128)}, u32[]{:S(2)}) copy-start(f32[2,1,64]{2,1,0:T(1,128)} %param.20) | copy-start | bytes 1540
  9.0 3.2 %copy-start.7 = (f32[64]{0:T(128)S(1)}, f32[64]{0:T(128)}, u32[]{:S(2)}) copy-start(f32[64]{0:T(128)} %param.22) | copy-start | bytes 772
  15.2 5.2 %copy-start.3 = (bf16[2,1,64]{2,0,1:T(2,128)(2,1)S(1)}, bf16[2,1,64]{2,0,1:T(2,128)(2,1)}, u32[]{:S(2)}) copy-start(bf16[2,1,64]{2,0,1:T(2,128)(2,1)} %param.19) | copy-start | bytes 772
  17.3 10.0 %copy-start.6 = (f32[64]{0:T(128)S(1)}, f32[64]{0:T(128)}, u32[]{:S(2)}) copy-start(f32[64]{0:T(128)} %param.23) | copy-start | bytes 772
  22.9 49.4 %copy-start.8 = (bf16[2,1,2]{2,0,1:T(2,128)(2,1)S(1)}, bf16[2,1,2]{2,0,1:T(2,128)(2,1)}, u32[]{:S(2)}) copy-start(bf16[2,1,2]{2,0,1:T(2,128)(2,1)} %param.29) | copy-start | bytes 28
  22.9 49.4 %copy-start.5 = (s32[2,1,2]{2,1,0:T(1,128)S(1)}, s32[2,1,2]{2,1,0:T(1,128)}, u32[]{:S(2)}) copy-start(s32[2,1,2]{2,1,0:T(1,128)} %param.28) | copy-start | bytes 52
  22.9 70.8 %copy-start.1 = (bf16[2,1,4096]{2,0,1:T(2,128)(2,1)S(1)}, bf16[2,1,4096]{2,0,1:T(2,128)(2,1)}, u32[]{:S(2)}) copy-start(bf16[2,1,4096]{2,0,1:T(2,128)(2,1)} %param.15) | copy-start | bytes 49156
  23.0 70.9 %copy-start = (f32[4096]{0:T(1024)S(1)}, f32[4096]{0:T(1024)}, u32[]{:S(2)}) copy-start(f32[4096]{0:T(1024)} %param.25) | copy-start | bytes 49156
  66.8 26.9 %all-to-all-start = ((f32[2,8,512]{2,0,1:T(2,128)}), f32[2,8,512]{2,0,1:T(2,128)S(1)}, u32[]{:S(2)}, u32[]{:S(2)}) async-start(f32[2,8,512]{2,0,1:T(2,128)} %copy.35), calls=%async_computation | async-start | bytes 65536 | tf_op jit(solution)/shard_map/all_to_all | solution.py:26
  72.3 145.2 %all-reduce.3.cloned.1.call-start = ((), (), s32[]{:S(2)}) async-start(), calls=%async_computation.1 | async-start | bytes 524288
  124.7 24.8 %copy-start.9 = (u32[32]{0:T(128)S(1)}, u32[32]{0:T(128)}, u32[]{:S(2)}) copy-start(u32[32]{0:T(128)} %constant.57) | copy-start | bytes 388
Sparse Core Ops, SparseCore 0:
  149.6 67.8 all-reduce.2
where the time goes:
time: 230 us
  blocking collectives  90.6 us (39%)
  waiting for transfers between devices  67.5 us (29%)
  matrix products  33.4 us (15%)
  local copies, waits for them, and re-layouts  13.9 us (6%)
  between operations  13.6 us (6%)
  starting transfers between devices  5.5 us (2%)
  other arithmetic  5.36 us (2%)
    unnamed x2, waiting for transfers between devices  67.4 us
    all_gather x1, blocking collectives, finish(): lax.all_gather(mixer, 'expert', axis=1, tiled=True)  32.3 us
    all_gather x1, blocking collectives, finish(): lax.all_gather(normed, 'expert', axis=1, tiled=True)  30.7 us
    dot_general x1, matrix products, finish(): jnp.einsum('tsc,cd->tsd', hidden, down_weight, preferred_element_type=jnp...  23.8 us
    all_gather x1, blocking collectives, finish(): lax.all_gather(table, 'expert', axis=1, tiled=True)  20.8 us
    dot_general x2, matrix products, on_device(): jnp.einsum('thpn,tn->thp', state, query, precision=lax.Precision.HIGHEST)  6.71 us
    all_to_all x1, starting transfers between devices, finish(): lax.all_to_all(summed, 'expert', split_axis=1, concat_axis=2, tiled=True)  5.46 us
    add x2, local copies, waits for them, and re-layouts, on_device(): factor[:, :, None, None] * state  5.14 us
  transfers between devices with their start and end apart: 2, of which 1 were waited for; matrix products, arithmetic and copies ran while one was open for 0% of the time, Pallas kernels for 0%

commit v1 on v0

--- a/solution.py
+++ b/solution.py
@@ -1,6 +1,9 @@
+import functools
 import jax
 import jax.numpy as jnp
 from jax import lax
+from jax.experimental import pallas as pl
+from jax.experimental.pallas import tpu as pltpu
 from jax.sharding import PartitionSpec as P
 
 P_SIZE = 64
@@ -55,6 +58,263 @@
     )
     total = lax.psum(combined, "head")
     return (wide + jnp.transpose(total, (1, 0, 2))).astype(jnp.bfloat16)
+
+
+LANES = 128
+WIDE = 512
+RING = 13
+
+
+def layer_kernel(
+    n,
+    mixer_ref, aux_ref, gain_ref, out_w, up_w, down_w,
+    total_ref, middle_ref,
+    ring, mixers, auxes, unpacked, rows, mine, theirs, blocks, normed, wide, hidden,
+    stage, packed, parts, halves,
+    weight_sem, mix_send, mix_recv, aux_send, aux_recv, core_send, core_recv,
+    mid_send, mid_recv, part_send, part_recv, half_send, half_recv,
+):
+    me = lax.axis_index("expert")
+    other = 1 - lax.axis_index("head")
+    ups = up_w.shape[1] // WIDE
+    downs = down_w.shape[1] // WIDE
+    pairs = downs // 2
+    columns = n * WIDE
+
+    def block(i):
+        return pl.ds(pl.multiple_of(i * WIDE, WIDE), WIDE)
+
+    def out_copy():
+        return pltpu.make_async_copy(out_w, ring.at[0], weight_sem.at[0])
+
+    def up_copy(i):
+        return pltpu.make_async_copy(up_w.at[:, block(i)], ring.at[1 + i], weight_sem.at[1 + i])
+
+    def down_copy(i):
+        at = 1 + ups + i
+        return pltpu.make_async_copy(
+            down_w.at[:, block(i)], ring.at[lax.rem(at, RING)], weight_sem.at[at]
+        )
+
+    early = RING - 1 - ups
+    out_copy().start()
+    pl.loop(0, ups)(lambda i: up_copy(i).start())
+    pl.loop(0, early)(lambda i: down_copy(i).start())
+
+    barrier = pltpu.get_barrier_semaphore()
+    for d in range(1, n):
+        pl.semaphore_signal(
+            barrier, inc=1, device_id={"expert": lax.rem(me + d, n)},
+            device_id_type=pl.DeviceIdType.MESH,
+        )
+    pl.semaphore_signal(
+        barrier, inc=1, device_id={"head": other}, device_id_type=pl.DeviceIdType.MESH
+    )
+    pl.semaphore_wait(barrier, n)
+
+    def to_peer(d, src, dst, send, recv):
+        return pltpu.make_async_remote_copy(
+            src_ref=src, dst_ref=dst, send_sem=send, recv_sem=recv,
+            device_id={"expert": lax.rem(me + d, n)}, device_id_type=pl.DeviceIdType.MESH,
+        )
+
+    def to_core(src, dst, send, recv):
+        return pltpu.make_async_remote_copy(
+            src_ref=src, dst_ref=dst, send_sem=send, recv_sem=recv,
+            device_id={"head": other}, device_id_type=pl.DeviceIdType.MESH,
+        )
+
+    mix = [
+        to_peer(d, mixer_ref, mixers.at[me], mix_send.at[d], mix_recv.at[d]) for d in range(1, n)
+    ]
+    aux = [
+        to_peer(d, aux_ref.at[lax.rem(me + d, n)], auxes.at[me], aux_send.at[d], aux_recv.at[d])
+        for d in range(1, n)
+    ]
+    for copy in mix + aux:
+        copy.start()
+    mixers[me] = mixer_ref[...]
+    auxes[me] = aux_ref[me]
+    for copy in mix:
+        copy.wait()
+    unpacked[...] = mixers[...].astype(jnp.float32)
+    for step in range(STEPS):
+        for k in range(n):
+            rows[step * n : (step + 1) * n, k * WIDE : (k + 1) * WIDE] = unpacked[:, step * n + k, :]
+
+    out_copy().wait()
+    mine[...] = jnp.dot(
+        rows[...].astype(jnp.bfloat16), ring[0], preferred_element_type=jnp.float32
+    )
+    down_copy(early).start()
+    swap = to_core(mine, theirs, core_send, core_recv)
+    swap.start()
+    for copy in aux:
+        copy.wait()
+    swap.wait()
+    per = WIDE // LANES
+    for step in range(STEPS):
+        for q in range(per):
+            at = slice(step * n, (step + 1) * n), slice(q * LANES, (q + 1) * LANES)
+            mine[at] = auxes[:, step * per + q, :] + (mine[at] + theirs[at])
+    blocks[me] = mine[...].astype(jnp.bfloat16)
+    mid = [
+        to_peer(d, blocks.at[me], blocks.at[me], mid_send.at[d], mid_recv.at[d])
+        for d in range(1, n)
+    ]
+    for copy in mid:
+        copy.start()
+    for copy in mid:
+        copy.wait()
+    square = jnp.zeros((STEPS * n, WIDE), jnp.float32)
+    for k in range(n):
+        part = blocks[k].astype(jnp.float32)
+        wide[:, k * WIDE : (k + 1) * WIDE] = part
+        square += part * part
+    scale = lax.rsqrt(jnp.sum(square, axis=-1, keepdims=True) / columns + EPSILON)
+    for k in range(n):
+        at = slice(None), slice(k * WIDE, (k + 1) * WIDE)
+        normed[at] = (wide[at] * scale * gain_ref[:, k * WIDE : (k + 1) * WIDE]).astype(jnp.bfloat16)
+    for step in range(STEPS):
+        middle_ref[step : step + 1, :] = wide[pl.ds(step * n + me, 1), :]
+    first = STEPS * per
+    weight = jnp.concatenate(
+        [auxes[:, first + step, :] for step in range(STEPS)], axis=0
+    )
+    weight = jnp.concatenate([weight] * per, axis=1)
+
+    @pl.loop(0, ups)
+    def _(i):
+        up_copy(i).wait()
+        x = jnp.dot(normed[...], ring[1 + i], preferred_element_type=jnp.float32)
+        inner = 0.7978845608028654 * (x + 0.044715 * (x * x * x))
+        hidden[:, block(i)] = ((x * (0.5 * (1.0 + jnp.tanh(inner)))) * weight).astype(jnp.bfloat16)
+
+        @pl.when(i < downs - early - 1)
+        def _():
+            down_copy(early + 1 + i).start()
+
+    def sends(pair):
+        return [
+            to_peer(
+                d, packed.at[pair, lax.rem(me + d, n)], parts.at[pair, me],
+                part_send.at[pair, d], part_recv.at[pair, d],
+            )
+            for d in range(1, n)
+        ]
+
+    @pl.loop(0, pairs)
+    def _(pair):
+        for half in range(2):
+            i = pair * 2 + half
+            down_copy(i).wait()
+            y = jnp.dot(
+                hidden[...], ring[lax.rem(1 + ups + i, RING)], preferred_element_type=jnp.float32
+            )
+            for step in range(STEPS):
+                for q in range(per):
+                    stage[:, (step * 2 + half) * per + q, :] = y[
+                        step * n : (step + 1) * n, q * LANES : (q + 1) * LANES
+                    ]
+        packed[pair] = stage[...].astype(jnp.bfloat16)
+        parts[pair, me] = packed[pair, me]
+        for copy in sends(pair):
+            copy.start()
+
+    @pl.loop(0, pairs)
+    def _(pair):
+        for copy in sends(pair):
+            copy.wait()
+        halves[0, pair] = jnp.sum(parts[pair].astype(jnp.float32), axis=0)
+
+    final = to_core(halves.at[0], halves.at[1], half_send, half_recv)
+    final.start()
+    final.wait()
+    total_ref[...] = halves[0] + halves[1]
+
+
+def fits(local_rows, mixer_width, columns, out_columns, hidden_width):
+    return (
+        local_rows == 1
+        and lax.axis_size("expert") * STEPS == 16
+        and lax.axis_size("head") == 2
+        and out_columns == WIDE
+        and mixer_width == columns == hidden_width == WIDE * lax.axis_size("expert")
+    )
+
+
+def in_kernel(mixer, stream, expert_ids, expert_gates, out_weight, norm_gain, up_weight, down_weight):
+    n = lax.axis_size("expert")
+    columns = stream.shape[2]
+    width = up_weight.shape[1]
+    downs = columns // WIDE
+    per = WIDE // LANES
+    table = jnp.sum(
+        jnp.where(
+            expert_ids[:, 0, :, None] == jnp.arange(EXPERTS)[None, None, :],
+            expert_gates[:, 0, :, None].astype(jnp.float32),
+            jnp.float32(0.0),
+        ),
+        axis=1,
+    )
+    target = (jnp.arange(n) * lax.axis_size("head") + lax.axis_index("head")) * width // FF
+    gates = jnp.sum(
+        jnp.where(target[:, None, None] == jnp.arange(EXPERTS), table[None], jnp.float32(0.0)), axis=2
+    )
+    lines = jnp.transpose(
+        stream.astype(jnp.float32).reshape(STEPS, n, per, LANES), (1, 0, 2, 3)
+    ).reshape(n, STEPS * per, LANES)
+    aux = jnp.concatenate(
+        [
+            lines,
+            jnp.broadcast_to(gates[:, :, None], (n, STEPS, LANES)),
+            jnp.zeros((n, 16 - STEPS * per - STEPS, LANES), jnp.float32),
+        ],
+        axis=1,
+    )
+    token = STEPS * n
+    vmem = pl.BlockSpec(memory_space=pltpu.VMEM)
+    hbm = pl.BlockSpec(memory_space=pl.ANY)
+    dma = pltpu.SemaphoreType.DMA
+    f32, bf16 = jnp.float32, jnp.bfloat16
+    total, middle = pl.pallas_call(
+        functools.partial(layer_kernel, n),
+        out_shape=(
+            jax.ShapeDtypeStruct((downs // 2, token, LANES), f32),
+            jax.ShapeDtypeStruct((STEPS, columns), f32),
+        ),
+        in_specs=[vmem, vmem, vmem, hbm, hbm, hbm],
+        out_specs=(vmem, vmem),
+        scratch_shapes=[
+            pltpu.VMEM((RING, columns, WIDE), bf16),
+            pltpu.VMEM((n, token, WIDE), bf16),
+            pltpu.VMEM((n, 16, LANES), f32),
+            pltpu.VMEM((n, token, WIDE), f32),
+            pltpu.VMEM((token, columns), f32),
+            pltpu.VMEM((token, WIDE), f32),
+            pltpu.VMEM((token, WIDE), f32),
+            pltpu.VMEM((n, token, WIDE), bf16),
+            pltpu.VMEM((token, columns), bf16),
+            pltpu.VMEM((token, columns), f32),
+            pltpu.VMEM((token, width), bf16),
+            pltpu.VMEM((n, token, LANES), f32),
+            pltpu.VMEM((downs // 2, n, token, LANES), bf16),
+            pltpu.VMEM((downs // 2, n, token, LANES), bf16),
+            pltpu.VMEM((2, downs // 2, token, LANES), f32),
+            dma((1 + width // WIDE + downs,)),
+            dma((n,)), dma((n,)), dma((n,)), dma((n,)), dma, dma,
+            dma((n,)), dma((n,)), dma((downs // 2, n)), dma((downs // 2, n)), dma, dma,
+        ],
+        compiler_params=pltpu.CompilerParams(
+            collective_id=0, has_side_effects=True, vmem_limit_bytes=60 << 20
+        ),
+    )(
+        mixer.reshape(token, WIDE), aux, norm_gain[None, :], out_weight, up_weight, down_weight
+    )
+    moe = jnp.transpose(
+        total.reshape(downs // 2, STEPS, 2 * per, LANES), (1, 0, 2, 3)
+    ).reshape(STEPS, 1, columns)
+    return (middle[:, None, :] + moe).astype(bf16)
 
 
 def on_device(
@@ -97,6 +357,17 @@
         )
         gate = heads_gate[step].astype(jnp.float32).reshape(local_rows, local_heads, P_SIZE)
         mixers.append((read * jax.nn.silu(gate)).reshape(local_rows, local_width).astype(jnp.bfloat16))
+    if fits(local_rows, local_width, stream.shape[2], out_weight.shape[1], up_weight.shape[1]):
+        return in_kernel(
+            jnp.stack(mixers),
+            stream,
+            expert_ids,
+            expert_gates,
+            out_weight,
+            norm_gain,
+            up_weight,
+            down_weight,
+        )
     return finish(
         jnp.stack(mixers),
         stream,

time: 230 us -> 57.8 us (0.25)
  blocking collectives: 90.6 us -> 0 us
  waiting for transfers between devices: 67.5 us -> 0 us
  Pallas kernels: 0 us -> 36.6 us
  matrix products: 33.4 us -> 5.07 us
  between operations: 13.6 us -> 0.17 us
  starting transfers between devices: 5.5 us -> 0 us
  local copies, waits for them, and re-layouts: 13.9 us -> 9.35 us
    all_gather x3 -> x0, blocking collectives: 83.8 us -> none  [the longest x1 32.3 us: finish(): lax.all_gather(mixer, 'expert', axis=1, tiled=True)]
    unnamed x2 -> x0, waiting for transfers between devices: 67.4 us -> none
    pallas_call x0 -> x1, Pallas kernels: none -> 36.6 us  [in_kernel(): pl.pallas_call(functools.partial(layer_kernel, n), out_shape=(jax.ShapeDt...]
    dot_general x2 -> x0, matrix products: 26.6 us -> none  [the longest x1 23.8 us: finish(): jnp.einsum('tsc,cd->tsd', hidden, down_weight, preferred_element_type=jnp...]
    psum x2 -> x0, blocking collectives: 6.8 us -> none  [the longest x1 3.41 us: finish(): summed = lax.psum(partial_out, 'head')]
    all_to_all x1 -> x0, starting transfers between devices: 5.46 us -> none  [finish(): lax.all_to_all(summed, 'expert', split_axis=1, concat_axis=2, tiled=True)]
  transfers between devices with their start and end apart: 2 -> 0, of which waited for: 1 -> 0; matrix products, arithmetic and copies ran while one was open for 0% -> 0% of each run, Pallas kernels for 0% -> 0%
where the time goes in v1:
time: 57.8 us; the launch traced here: 57.4 us
  Pallas kernels  36.6 us (63%)
  local copies, waits for them, and re-layouts  9.35 us (16%)
  other arithmetic  6.26 us (11%)
  matrix products  5.07 us (9%)
    pallas_call x1, Pallas kernels, in_kernel(): pl.pallas_call(functools.partial(layer_kernel, n), out_shape=(jax.ShapeDt...  36.6 us
    dot_general x2, matrix products, on_device(): jnp.einsum('thpn,tn->thp', state, query, precision=lax.Precision.HIGHEST)  5.07 us
    mul x8, local copies, waits for them, and re-layouts, on_device(): (delta[:, :, None] * values)[:, :, :, None] * keys[:, None, None, :]  3.67 us
    add x2, local copies, waits for them, and re-layouts, on_device(): factor[:, :, None, None] * state  2.86 us
    add x1, other arithmetic, on_device(): factor[:, :, None, None] * state  2.69 us
    convert_element_type x1, other arithmetic, in_kernel(): return (middle[:, None, :] + moe).astype(bf16)  1.4 us

profile of v1, /device:TPU:0, one launch (start us, length us, event | category | flops | bytes accessed | tf_op | source)
XLA Modules:
  0.0 57.4 jit_solution(13193974067805713547)
XLA Ops:
  0.0 1.0 %convert_reduce_fusion.2 = (f32[4096]{0:T(1024)S(1)}, f32[4096]{0:T(1024)S(1)}, f32[4096]{0:T(1024)S(1)}, f32[4096]{0:T(1024)S(1)}) fusion(bf16[2,1,4096]{2,0,1:T(2,128)(2,1)} %param.17, bf16[2,1,4096]{2,0,1:T(2,128)(2,1)} %param.16), kind=kLoop, calls=%fused_computation.12 | loop fusion | flops 16384 | bytes 98304 | tf_op jit(solution)/shard_map/convert_element_type | solution.py:358
  1.1 0.7 %slice_bitcast_fusion.1 = (f32[64]{0:T(128)S(1)}, f32[64]{0:T(128)S(1)}) fusion(f32[2,1,64]{2,1,0:T(1,128)} %param.20), kind=kLoop, calls=%fused_computation.36 | loop fusion | bytes 1024 | tf_op jit(solution)/shard_map/squeeze | solution.py:346
  1.8 0.6 %mul.176 = f32[64,64,64]{2,1,0:T(8,128)S(1)} broadcast(f32[64,64]{1,0:T(8,128)S(1)} %broadcast_multiply_fusion.1), dimensions={0,1} | broadcast | bytes 1064960 | tf_op jit(solution)/shard_map/mul | solution.py:352
  2.4 0.7 %mul.177 = f32[1,64,4096]{2,1,0:T(8,128)S(1)} reshape(f32[64,64,64]{2,1,0:T(8,128)S(1)} %mul.176) | data formatting | bytes 2097152 | tf_op jit(solution)/shard_map/mul | solution.py:352
  3.1 0.1 broadcast_multiply_fusion
  3.2 0.6 %mul.191 = f32[64,64,64]{2,1,0:T(8,128)S(1)} broadcast(f32[64,64]{1,0:T(8,128)S(1)} %broadcast_multiply_fusion), dimensions={0,1} | broadcast | bytes 1064960 | tf_op jit(solution)/shard_map/mul | solution.py:352
  3.9 1.6 %mul.192 = f32[1,64,4096]{2,1,0:T(8,128)} reshape(f32[64,64,64]{2,1,0:T(8,128)S(1)} %mul.191) | data formatting | bytes 2097152 | tf_op jit(solution)/shard_map/mul | solution.py:352
  5.7 2.7 %multiply_add_fusion = (f32[1,64,4096]{2,1,0:T(8,128)}, f32[1,64,4096]{2,1,0:T(8,128)S(1)}) fusion(f32[1,64,4096]{2,1,0:T(8,128)} %mul.192, f32[4096]{0:T(1024)S(1)} %mul.194, f32[64]{0:T(128)S(1)} %get-tuple-element.16, f32[1,64,4096]{2,1,0:T(8,128)S(1)} %mul.177, f32[4096]{0:T(1024)S(1)} %mul.179, bf16[1,64,4096]{2,1,0:T(8,128)(2,1)} %param.21, ...), kind=kLoop, calls=%fused_computation | loop fusion | flops 1835008 | bytes 4751872 | tf_op jit(solution)/shard_map/add | solution.py:351
  8.4 2.0 %add.62 = f32[64,64,64]{2,1,0:T(8,128)S(1)} reshape(f32[1,64,4096]{2,1,0:T(8,128)} %get-tuple-element.13) | data formatting | bytes 2097152 | tf_op jit(solution)/shard_map/add | solution.py:351
  10.4 2.5 %fusion.3 = f32[1,64,64]{2,0,1:T(1,128)S(1)} fusion(f32[64,64,64]{2,1,0:T(8,128)S(1)} %add.62, bf16[2,1,64]{2,0,1:T(2,128)(2,1)S(1)} %copy-done.2), kind=kOutput, calls=%fused_computation.25 | convolution fusion | flops 3145728 | bytes 1065216 | tf_op jit(solution)/shard_map/thpn,tn->thp/dot_general | solution.py:355
  12.9 0.9 %add.58 = f32[64,64,64]{2,1,0:T(8,128)S(1)} reshape(f32[1,64,4096]{2,1,0:T(8,128)S(1)} %get-tuple-element.14) | data formatting | bytes 2097152 | tf_op jit(solution)/shard_map/add | solution.py:351
  13.8 2.5 %fusion.5 = f32[1,64,64]{2,0,1:T(1,128)S(1)} fusion(f32[64,64,64]{2,1,0:T(8,128)S(1)} %add.58, bf16[2,1,64]{2,0,1:T(2,128)(2,1)S(1)} %copy-done.2), kind=kOutput, calls=%fused_computation.28 | convolution fusion | flops 3145728 | bytes 1065216 | tf_op jit(solution)/shard_map/thpn,tn->thp/dot_general | solution.py:355
  16.5 0.1 multiply_convert_fusion.1
  16.6 0.1 convert_element_type.135
  16.7 0.1 convert_element_type.143
  16.8 0.6 %reshape.360.mixer_ref = bf16[16,512]{1,0:T(8,128)(2,1)} reshape(bf16[2,1,4096]{2,0,1:T(2,128)(2,1)S(1)} %pad_maximum_fusion) | data formatting | bytes 32768 | tf_op jit(solution)/shard_map/reshape | solution.py:312
  17.6 0.1 fusion.2
  17.6 0.1 select_reduce_fusion
  17.7 0.1 copy.19
  17.9 0.1 pad.2.clone
  18.0 0.7 %maximum_maximum_fusion.aux_ref = f32[8,16,128]{2,1,0:T(8,128)} fusion(f32[8,2,128]{2,1,0:T(2,128)S(1)} %broadcast_in_dim.64, f32[8,8,128]{2,1,0:T(8,128)S(1)} %bitcast.59, f32[16]{0:T(128)S(1)} %pad.2.clone), kind=kLoop, calls=%fused_computation.2 | loop fusion | flops 32768 | bytes 106560 | tf_op jit(solution)/shard_map/concatenate | solution.py:267
  18.7 36.6 %shard_map.145 = (f32[4,16,128]{2,1,0:T(8,128)}, f32[2,4096]{1,0:T(2,128)}) custom-call(bf16[16,512]{1,0:T(8,128)(2,1)} %reshape.360.mixer_ref, f32[8,16,128]{2,1,0:T(8,128)} %maximum_maximum_fusion.aux_ref, f32[1,4096]{1,0:T(1,128)} %bitcast.60, bf16[4096,512]{1,0:T(8,128)(2,1)} %out_w.1, bf16[4096,4096]{1,0:T(8,128)(2,1)} %up_w.1, bf16[4096,4096]{1,0:T(8,128)(2,1)} %down_w.1), custom_call_target="tpu_custom_call" | custom-call | tf_op jit(solution)/shard_map/pallas_call | solution.py:280
  55.3 0.8 %copy_bitcast_fusion = f32[1,2,32,128]{3,2,1,0:T(8,128)S(1)} fusion(f32[4,16,128]{2,1,0:T(8,128)} %get-tuple-element.8), kind=kLoop, calls=%fused_computation.5 | loop fusion | bytes 65536
  56.0 1.4 %fusion.1 = bf16[2,1,4096]{2,0,1:T(2,128)(2,1)} fusion(f32[2,4096]{1,0:T(2,128)} %get-tuple-element.7, f32[1,2,32,128]{3,2,1,0:T(8,128)S(1)} %copy_bitcast_fusion), kind=kLoop, calls=%fused_computation.8 | loop fusion | flops 16384 | bytes 81920 | tf_op jit(solution)/shard_map/convert_element_type | solution.py:317
  (35 shorter events, 0.7 us)
Async XLA Ops:
  3.8 1.7 %copy-start.3 = (bf16[2,1,64]{2,0,1:T(2,128)(2,1)S(1)}, bf16[2,1,64]{2,0,1:T(2,128)(2,1)}, u32[]{:S(2)}) copy-start(bf16[2,1,64]{2,0,1:T(2,128)(2,1)} %param.18) | copy-start | bytes 772
  3.8 1.8 %copy-start.1 = (f32[2,1,64]{2,1,0:T(1,128)S(1)}, f32[2,1,64]{2,1,0:T(1,128)}, u32[]{:S(2)}) copy-start(f32[2,1,64]{2,1,0:T(1,128)} %param.20) | copy-start | bytes 1540
  3.8 1.8 %copy-start.6 = (f32[64]{0:T(128)S(1)}, f32[64]{0:T(128)}, u32[]{:S(2)}) copy-start(f32[64]{0:T(128)} %param.22) | copy-start | bytes 772
  8.4 2.0 %copy-start.2 = (bf16[2,1,64]{2,0,1:T(2,128)(2,1)S(1)}, bf16[2,1,64]{2,0,1:T(2,128)(2,1)}, u32[]{:S(2)}) copy-start(bf16[2,1,64]{2,0,1:T(2,128)(2,1)} %param.19) | copy-start | bytes 772
  12.9 3.6 %copy-start.5 = (f32[64]{0:T(128)S(1)}, f32[64]{0:T(128)}, u32[]{:S(2)}) copy-start(f32[64]{0:T(128)} %param.23) | copy-start | bytes 772
  12.9 4.5 %copy-start = (bf16[2,1,4096]{2,0,1:T(2,128)(2,1)S(1)}, bf16[2,1,4096]{2,0,1:T(2,128)(2,1)}, u32[]{:S(2)}) copy-start(bf16[2,1,4096]{2,0,1:T(2,128)(2,1)} %param.15) | copy-start | bytes 49156
  13.8 3.7 %copy-start.7 = (bf16[2,1,2]{2,0,1:T(2,128)(2,1)S(1)}, bf16[2,1,2]{2,0,1:T(2,128)(2,1)}, u32[]{:S(2)}) copy-start(bf16[2,1,2]{2,0,1:T(2,128)(2,1)} %param.29) | copy-start | bytes 28
  13.8 3.7 %copy-start.4 = (s32[2,1,2]{2,1,0:T(1,128)S(1)}, s32[2,1,2]{2,1,0:T(1,128)}, u32[]{:S(2)}) copy-start(s32[2,1,2]{2,1,0:T(1,128)} %param.28) | copy-start | bytes 52

commit v2 on v1

--- a/solution.py
+++ b/solution.py
@@ -67,11 +67,11 @@
 
 def layer_kernel(
     n,
-    mixer_ref, aux_ref, gain_ref, out_w, up_w, down_w,
+    facts_ref, values_ref, gate_ref, aux_ref, gain_ref, state_in, out_w, up_w, down_w,
     total_ref, middle_ref,
-    ring, mixers, auxes, unpacked, rows, mine, theirs, blocks, normed, wide, hidden,
+    state, queries, spread, lines, mixed, mixer_ref, ring, mixers, auxes, unpacked, rows, mine, theirs, blocks, normed, wide, hidden,
     stage, packed, parts, halves,
-    weight_sem, mix_send, mix_recv, aux_send, aux_recv, core_send, core_recv,
+    state_sem, weight_sem, mix_send, mix_recv, aux_send, aux_recv, core_send, core_recv,
     mid_send, mid_recv, part_send, part_recv, half_send, half_recv,
 ):
     me = lax.axis_index("expert")
@@ -96,6 +96,8 @@
             down_w.at[:, block(i)], ring.at[lax.rem(at, RING)], weight_sem.at[at]
         )
 
+    state_copy = pltpu.make_async_copy(state_in, state, state_sem)
+    state_copy.start()
     early = RING - 1 - ups
     out_copy().start()
     pl.loop(0, ups)(lambda i: up_copy(i).start())
@@ -110,6 +112,64 @@
     pl.semaphore_signal(
         barrier, inc=1, device_id={"head": other}, device_id_type=pl.DeviceIdType.MESH
     )
+
+    heads, half = facts_ref.shape[1], P_SIZE
+    eye = lax.broadcasted_iota(jnp.int32, (heads, heads), 0) == lax.broadcasted_iota(
+        jnp.int32, (heads, heads), 1
+    )
+
+    def column(row):
+        return jnp.sum(jnp.where(eye, facts_ref[row : row + 1, :], 0.0), axis=1, keepdims=True)
+
+    def meet(key, query):
+        return jnp.sum(
+            facts_ref[4 + key : 5 + key, :] * facts_ref[6 + query : 7 + query, :],
+            axis=1, keepdims=True,
+        )
+
+    lane = lax.broadcasted_iota(jnp.int32, (heads, 2 * half), 1)
+    before = lane < half
+
+    def both(a, b):
+        return jnp.where(before, a, b)
+
+    query = both(column(6), column(7))
+    place = lax.rem(lane, half)
+    for p in range(P_SIZE):
+        queries[p * N : (p + 1) * N, :] = jnp.where(place == p, query, 0.0).astype(jnp.bfloat16)
+    delta0, delta1, decay, skip = column(0), column(1), column(2), column(3)
+    factor0, factor1 = jnp.exp(-delta0 * decay), jnp.exp(-delta1 * decay)
+    spread[heads : 2 * heads, :] = both(delta0 * meet(0, 0) + skip, delta1 * meet(1, 1) + skip)
+    spread[2 * heads : 3 * heads, :] = both(skip * 0.0, factor1 * delta0 * meet(0, 1))
+    for at, source in enumerate((values_ref, gate_ref)):
+        for step in range(STEPS):
+            for k in range(n):
+                lines[at, step * n + k : step * n + k + 1, :] = source[
+                    step : step + 1, k * WIDE : (k + 1) * WIDE
+                ].astype(jnp.float32)
+    state_copy.wait()
+    spread[0:heads, :] = jnp.dot(
+        state[...], queries[...], preferred_element_type=jnp.float32
+    ) * both(factor0, factor0 * factor1)
+    for j in range(WIDE // LANES):
+
+        def pick(kind):
+            even = spread[pl.ds(kind * heads + 2 * j, n, stride=WIDE // P_SIZE), :]
+            odd = spread[pl.ds(kind * heads + 2 * j + 1, n, stride=WIDE // P_SIZE), :]
+            return (
+                jnp.concatenate([even[:, :half], odd[:, :half]], axis=1),
+                jnp.concatenate([even[:, half:], odd[:, half:]], axis=1),
+            )
+
+        at = slice(j * LANES, (j + 1) * LANES)
+        read, own, past = pick(0), pick(1), pick(2)
+        value0, value1 = lines[0, 0:n, at], lines[0, n : 2 * n, at]
+        gate0, gate1 = lines[1, 0:n, at], lines[1, n : 2 * n, at]
+        mixed[0:n, at] = (read[0] + own[0] * value0) * (gate0 / (1.0 + jnp.exp(-gate0)))
+        mixed[n : 2 * n, at] = (read[1] + own[1] * value1 + past[1] * value0) * (
+            gate1 / (1.0 + jnp.exp(-gate1))
+        )
+    mixer_ref[...] = mixed[...].astype(jnp.bfloat16)
     pl.semaphore_wait(barrier, n)
 
     def to_peer(d, src, dst, send, recv):
@@ -243,7 +303,23 @@
     )
 
 
-def in_kernel(mixer, stream, expert_ids, expert_gates, out_weight, norm_gain, up_weight, down_weight):
+def in_kernel(
+    stream,
+    heads_in,
+    heads_gate,
+    write_key,
+    read_query,
+    step_size,
+    state_cache,
+    decay_rate,
+    skip_gain,
+    out_weight,
+    norm_gain,
+    up_weight,
+    down_weight,
+    expert_ids,
+    expert_gates,
+):
     n = lax.axis_size("expert")
     columns = stream.shape[2]
     width = up_weight.shape[1]
@@ -273,6 +349,17 @@
         axis=1,
     )
     token = STEPS * n
+    heads = decay_rate.shape[0]
+    facts = jnp.concatenate(
+        [
+            step_size[:, 0],
+            decay_rate[None],
+            skip_gain[None],
+            write_key[:, 0].astype(jnp.float32),
+            read_query[:, 0].astype(jnp.float32),
+        ],
+        axis=0,
+    )
     vmem = pl.BlockSpec(memory_space=pltpu.VMEM)
     hbm = pl.BlockSpec(memory_space=pl.ANY)
     dma = pltpu.SemaphoreType.DMA
@@ -283,9 +370,15 @@
             jax.ShapeDtypeStruct((downs // 2, token, LANES), f32),
             jax.ShapeDtypeStruct((STEPS, columns), f32),
         ),
-        in_specs=[vmem, vmem, vmem, hbm, hbm, hbm],
+        in_specs=[vmem, vmem, vmem, vmem, vmem, hbm, hbm, hbm, hbm],
         out_specs=(vmem, vmem),
         scratch_shapes=[
+            pltpu.VMEM((heads, P_SIZE * N), bf16),
+            pltpu.VMEM((P_SIZE * N, STEPS * P_SIZE), bf16),
+            pltpu.VMEM((3 * heads, STEPS * P_SIZE), f32),
+            pltpu.VMEM((2, token, WIDE), f32),
+            pltpu.VMEM((token, WIDE), f32),
+            pltpu.VMEM((token, WIDE), bf16),
             pltpu.VMEM((RING, columns, WIDE), bf16),
             pltpu.VMEM((n, token, WIDE), bf16),
             pltpu.VMEM((n, 16, LANES), f32),
@@ -301,6 +394,7 @@
             pltpu.VMEM((downs // 2, n, token, LANES), bf16),
             pltpu.VMEM((downs // 2, n, token, LANES), bf16),
             pltpu.VMEM((2, downs // 2, token, LANES), f32),
+            dma,
             dma((1 + width // WIDE + downs,)),
             dma((n,)), dma((n,)), dma((n,)), dma((n,)), dma, dma,
             dma((n,)), dma((n,)), dma((downs // 2, n)), dma((downs // 2, n)), dma, dma,
@@ -309,7 +403,8 @@
             collective_id=0, has_side_effects=True, vmem_limit_bytes=60 << 20
         ),
     )(
-        mixer.reshape(token, WIDE), aux, norm_gain[None, :], out_weight, up_weight, down_weight
+        facts, heads_in[:, 0], heads_gate[:, 0], aux, norm_gain[None, :], state_cache[0],
+        out_weight, up_weight, down_weight,
     )
     moe = jnp.transpose(
         total.reshape(downs // 2, STEPS, 2 * per, LANES), (1, 0, 2, 3)
@@ -337,6 +432,24 @@
     local_rows = heads_in.shape[1]
     local_width = heads_in.shape[2]
     local_heads = decay_rate.shape[0]
+    if fits(local_rows, local_width, stream.shape[2], out_weight.shape[1], up_weight.shape[1]):
+        return in_kernel(
+            stream,
+            heads_in,
+            heads_gate,
+            write_key,
+            read_query,
+            step_size,
+            state_cache,
+            decay_rate,
+            skip_gain,
+            out_weight,
+            norm_gain,
+            up_weight,
+            down_weight,
+            expert_ids,
+            expert_gates,
+        )
     state = state_cache.astype(jnp.float32).reshape(local_rows, local_heads, P_SIZE, N)
     position = lax.axis_index("expert") * lax.axis_size("head") + lax.axis_index("head")
     owner = position * up_weight.shape[1] // FF
@@ -357,17 +470,6 @@
         )
         gate = heads_gate[step].astype(jnp.float32).reshape(local_rows, local_heads, P_SIZE)
         mixers.append((read * jax.nn.silu(gate)).reshape(local_rows, local_width).astype(jnp.bfloat16))
-    if fits(local_rows, local_width, stream.shape[2], out_weight.shape[1], up_weight.shape[1]):
-        return in_kernel(
-            jnp.stack(mixers),
-            stream,
-            expert_ids,
-            expert_gates,
-            out_weight,
-            norm_gain,
-            up_weight,
-            down_weight,
-        )
     return finish(
         jnp.stack(mixers),
         stream,

time: 57.8 us -> 44.4 us (0.77)
  local copies, waits for them, and re-layouts: 9.35 us -> 3.04 us
  matrix products: 5.07 us -> 0 us
  other arithmetic: 6.26 us -> 4.3 us
    dot_general x2 -> x0, matrix products: 5.07 us -> none  [on_device(): jnp.einsum('thpn,tn->thp', state, query, precision=lax.Precision.HIGHEST)]
    mul x8 -> x0, local copies, waits for them, and re-layouts: 3.67 us -> none  [on_device(): (delta[:, :, None] * values)[:, :, :, None] * keys[:, None, None, :]]
    add x2 -> x0, local copies, waits for them, and re-layouts: 2.86 us -> none  [on_device(): factor[:, :, None, None] * state]
    add x1 -> x0, other arithmetic: 2.69 us -> none  [on_device(): factor[:, :, None, None] * state]
    concatenate x0 -> x1, local copies, waits for them, and re-layouts: none -> 1.3 us  [in_kernel(): jnp.concatenate([step_size[:, 0], decay_rate[None], skip_gain[None], writ...]
    reshape x2, local copies, waits for them, and re-layouts: 0.03 us -> 0.75 us  [in_kernel(): lines = jnp.transpose(stream.astype(jnp.float32).reshape(STEPS, n, per, L...]
    reduce_sum x1, other arithmetic: 0.09 us -> 0.76 us  [in_kernel(): jnp.sum(jnp.where(expert_ids[:, 0, :, None] == jnp.arange(EXPERTS)[None,...]
    squeeze x1 -> x0, local copies, waits for them, and re-layouts: 0.67 us -> none  [on_device(): delta = step_size[step]]
where the time goes in v2:
time: 44.4 us; the launch traced here: 44 us
  Pallas kernels  36.6 us (82%)
  other arithmetic  4.3 us (10%)
  local copies, waits for them, and re-layouts  3.04 us (7%)
    pallas_call x1, Pallas kernels, in_kernel(): pl.pallas_call(functools.partial(layer_kernel, n), out_shape=(jax.ShapeDt...  36.6 us
    convert_element_type x1, other arithmetic, in_kernel(): return (middle[:, None, :] + moe).astype(bf16)  1.4 us
    concatenate x1, local copies, waits for them, and re-layouts, in_kernel(): jnp.concatenate([step_size[:, 0], decay_rate[None], skip_gain[None], writ...  1.3 us

profile of v2, /device:TPU:0, one launch (start us, length us, event | category | flops | bytes accessed | tf_op | source)
XLA Modules:
  0.0 44.0 jit_solution(15730294204923435934)
XLA Ops:
  0.0 0.1 pad.2.clone
  0.1 0.7 %bitcast_convert_fusion = f32[2,2]{1,0:T(2,128)S(1)} fusion(bf16[2,1,2]{2,0,1:T(2,128)(2,1)} %param.29), kind=kLoop, calls=%fused_computation.13 | loop fusion | flops 4 | bytes 24 | tf_op jit(solution)/shard_map/convert_element_type | solution.py:331
  0.8 0.8 %fusion.2 = f32[2,4]{1,0:T(2,128)S(1)} fusion(f32[2,2]{1,0:T(2,128)S(1)} %bitcast_convert_fusion, s32[2,2]{1,0:T(2,128)} %bitcast.42), kind=kLoop, calls=%fused_computation.7 | loop fusion | flops 40 | bytes 64 | tf_op jit(solution)/shard_map/reduce_sum | solution.py:328
  1.5 0.1 select_reduce_fusion
  1.6 0.7 %bitcast_convert_fusion.1 = (f32[2,64]{1,0:T(2,128)S(1)}, f32[2,64]{1,0:T(2,128)S(1)}) fusion(bf16[2,1,64]{2,0,1:T(2,128)(2,1)} %param.19, bf16[2,1,64]{2,0,1:T(2,128)(2,1)} %param.18), kind=kLoop, calls=%fused_computation.14 | loop fusion | flops 256 | bytes 1536 | tf_op jit(solution)/shard_map/convert_element_type | solution.py:359
  2.3 1.3 %concatenate.6.facts_ref = f32[8,64]{1,0:T(8,128)} concatenate(f32[2,64]{1,0:T(2,128)} %bitcast.43, f32[1,64]{1,0:T(1,128)} %bitcast.44, f32[1,64]{1,0:T(1,128)} %bitcast.45, f32[2,64]{1,0:T(2,128)S(1)} %get-tuple-element.10, f32[2,64]{1,0:T(2,128)S(1)} %get-tuple-element.9), dimensions={0} | concatenate | bytes 4096 | tf_op jit(solution)/shard_map/concatenate | solution.py:353
  3.6 0.1 copy.19
  3.7 0.1 broadcast_in_dim.62
  3.8 0.7 %reshape.90 = f32[2,8,4,128]{3,2,1,0:T(4,128)S(1)} reshape(bf16[2,1,4096]{2,0,1:T(2,128)(2,1)} %param.15) | data formatting | bytes 49152 | tf_op jit(solution)/shard_map/reshape | solution.py:342
  4.5 0.7 %maximum_maximum_fusion.aux_ref = f32[8,16,128]{2,1,0:T(8,128)} fusion(f32[8,2,128]{2,1,0:T(2,128)S(1)} %broadcast_in_dim.62, f32[8,8,128]{2,1,0:T(8,128)S(1)} %bitcast.38, f32[16]{0:T(128)S(1)} %pad.2.clone), kind=kLoop, calls=%fused_computation | loop fusion | flops 32768 | bytes 106560 | tf_op jit(solution)/shard_map/concatenate | solution.py:343
  5.2 36.6 %shard_map.145 = (f32[4,16,128]{2,1,0:T(8,128)}, f32[2,4096]{1,0:T(2,128)}) custom-call(f32[8,64]{1,0:T(8,128)} %concatenate.6.facts_ref, bf16[2,4096]{1,0:T(2,128)(2,1)} %bitcast.39, bf16[2,4096]{1,0:T(2,128)(2,1)} %bitcast.40, f32[8,16,128]{2,1,0:T(8,128)} %maximum_maximum_fusion.aux_ref, f32[1,4096]{1,0:T(1,128)} %bitcast.41, bf16[64,4096]{1,0:T(8,128)(2,1)} %bitcast.37, ...), custom_call_target="tpu_custom_call" | custom-call | tf_op jit(solution)/shard_map/pallas_call | solution.py:367
  41.8 0.8 %copy_bitcast_fusion = f32[1,2,32,128]{3,2,1,0:T(8,128)S(1)} fusion(f32[4,16,128]{2,1,0:T(8,128)} %get-tuple-element.8), kind=kLoop, calls=%fused_computation.3 | loop fusion | bytes 65536
  42.6 1.4 %fusion.1 = bf16[2,1,4096]{2,0,1:T(2,128)(2,1)} fusion(f32[2,4096]{1,0:T(2,128)} %get-tuple-element.7, f32[1,2,32,128]{3,2,1,0:T(8,128)S(1)} %copy_bitcast_fusion), kind=kLoop, calls=%fused_computation.4 | loop fusion | flops 16384 | bytes 81920 | tf_op jit(solution)/shard_map/convert_element_type | solution.py:412
  (4 shorter events, 0.0 us)

commit v3 on v2

--- a/solution.py
+++ b/solution.py
@@ -67,8 +67,10 @@
 
 def layer_kernel(
     n,
-    facts_ref, values_ref, gate_ref, aux_ref, gain_ref, state_in, out_w, up_w, down_w,
-    total_ref, middle_ref,
+    delta_ref, decay_ref, skip_ref, key_ref, query_ref, stream_ref, ids_ref, gates_ref,
+    values_ref, gate_ref, gain_ref, state_in, out_w, up_w, down_w,
+    out_ref,
+    facts_ref, aux_ref, middle_ref,
     state, queries, spread, lines, mixed, mixer_ref, ring, mixers, auxes, unpacked, rows, mine, theirs, blocks, normed, wide, hidden,
     stage, packed, parts, halves,
     state_sem, weight_sem, mix_send, mix_recv, aux_send, aux_recv, core_send, core_recv,
@@ -114,6 +116,26 @@
     )
 
     heads, half = facts_ref.shape[1], P_SIZE
+    facts_ref[0:2, :] = delta_ref[...]
+    facts_ref[2:3, :] = decay_ref[...]
+    facts_ref[3:4, :] = skip_ref[...]
+    facts_ref[4:6, :] = key_ref[...].astype(jnp.float32)
+    facts_ref[6:8, :] = query_ref[...].astype(jnp.float32)
+    quarter = WIDE // LANES
+    aux_ref[...] = jnp.zeros_like(aux_ref)
+    entering = stream_ref[...].astype(jnp.float32)
+    chosen = gates_ref[...].astype(jnp.float32)
+    for k in range(n):
+        for step in range(STEPS):
+            for q in range(quarter):
+                first = k * WIDE + q * LANES
+                at = step * quarter + q
+                aux_ref[k, at : at + 1, :] = entering[step : step + 1, first : first + LANES]
+        expert = (k * 2 + lax.axis_index("head")) * up_w.shape[1] // FF
+        given = jnp.sum(jnp.where(ids_ref[...] == expert, chosen, 0.0), axis=1, keepdims=True)
+        aux_ref[k, STEPS * quarter : STEPS * quarter + STEPS, :] = jnp.broadcast_to(
+            given.astype(jnp.bfloat16).astype(jnp.float32), (STEPS, LANES)
+        )
     eye = lax.broadcasted_iota(jnp.int32, (heads, heads), 0) == lax.broadcasted_iota(
         jnp.int32, (heads, heads), 1
     )
@@ -290,7 +312,15 @@
     final = to_core(halves.at[0], halves.at[1], half_send, half_recv)
     final.start()
     final.wait()
-    total_ref[...] = halves[0] + halves[1]
+    for pair in range(downs // 2):
+        both_cores = halves[0, pair] + halves[1, pair]
+        for step in range(STEPS):
+            for q in range(2 * per):
+                first = (pair * 2 * per + q) * LANES
+                at = slice(step, step + 1), slice(first, first + LANES)
+                line = step * 2 * per + q
+                middle_ref[at] = middle_ref[at] + both_cores[line : line + 1, :]
+    out_ref[...] = middle_ref[...].astype(jnp.bfloat16)
 
 
 def fits(local_rows, mixer_width, columns, out_columns, hidden_width):
@@ -324,55 +354,21 @@
     columns = stream.shape[2]
     width = up_weight.shape[1]
     downs = columns // WIDE
-    per = WIDE // LANES
-    table = jnp.sum(
-        jnp.where(
-            expert_ids[:, 0, :, None] == jnp.arange(EXPERTS)[None, None, :],
-            expert_gates[:, 0, :, None].astype(jnp.float32),
-            jnp.float32(0.0),
-        ),
-        axis=1,
-    )
-    target = (jnp.arange(n) * lax.axis_size("head") + lax.axis_index("head")) * width // FF
-    gates = jnp.sum(
-        jnp.where(target[:, None, None] == jnp.arange(EXPERTS), table[None], jnp.float32(0.0)), axis=2
-    )
-    lines = jnp.transpose(
-        stream.astype(jnp.float32).reshape(STEPS, n, per, LANES), (1, 0, 2, 3)
-    ).reshape(n, STEPS * per, LANES)
-    aux = jnp.concatenate(
-        [
-            lines,
-            jnp.broadcast_to(gates[:, :, None], (n, STEPS, LANES)),
-            jnp.zeros((n, 16 - STEPS * per - STEPS, LANES), jnp.float32),
-        ],
-        axis=1,
-    )
     token = STEPS * n
     heads = decay_rate.shape[0]
-    facts = jnp.concatenate(
-        [
-            step_size[:, 0],
-            decay_rate[None],
-            skip_gain[None],
-            write_key[:, 0].astype(jnp.float32),
-            read_query[:, 0].astype(jnp.float32),
-        ],
-        axis=0,
-    )
     vmem = pl.BlockSpec(memory_space=pltpu.VMEM)
     hbm = pl.BlockSpec(memory_space=pl.ANY)
     dma = pltpu.SemaphoreType.DMA
     f32, bf16 = jnp.float32, jnp.bfloat16
-    total, middle = pl.pallas_call(
+    result = pl.pallas_call(
         functools.partial(layer_kernel, n),
-        out_shape=(
-            jax.ShapeDtypeStruct((downs // 2, token, LANES), f32),
-            jax.ShapeDtypeStruct((STEPS, columns), f32),
-        ),
-        in_specs=[vmem, vmem, vmem, vmem, vmem, hbm, hbm, hbm, hbm],
-        out_specs=(vmem, vmem),
+        out_shape=jax.ShapeDtypeStruct((STEPS, columns), bf16),
+        in_specs=[vmem] * 11 + [hbm] * 4,
+        out_specs=vmem,
         scratch_shapes=[
+            pltpu.VMEM((8, heads), f32),
+            pltpu.VMEM((n, 16, LANES), f32),
+            pltpu.VMEM((STEPS, columns), f32),
             pltpu.VMEM((heads, P_SIZE * N), bf16),
             pltpu.VMEM((P_SIZE * N, STEPS * P_SIZE), bf16),
             pltpu.VMEM((3 * heads, STEPS * P_SIZE), f32),
@@ -403,13 +399,11 @@
             collective_id=0, has_side_effects=True, vmem_limit_bytes=60 << 20
         ),
     )(
-        facts, heads_in[:, 0], heads_gate[:, 0], aux, norm_gain[None, :], state_cache[0],
+        step_size[:, 0], decay_rate[None], skip_gain[None], write_key[:, 0], read_query[:, 0],
+        stream[:, 0], expert_ids[:, 0], expert_gates[:, 0], heads_in[:, 0], heads_gate[:, 0], norm_gain[None, :], state_cache[0],
         out_weight, up_weight, down_weight,
     )
-    moe = jnp.transpose(
-        total.reshape(downs // 2, STEPS, 2 * per, LANES), (1, 0, 2, 3)
-    ).reshape(STEPS, 1, columns)
-    return (middle[:, None, :] + moe).astype(bf16)
+    return result[:, None, :]
 
 
 def on_device(

time: 44.4 us -> 38.4 us (0.86)
  other arithmetic: 4.3 us -> 0 us
  local copies, waits for them, and re-layouts: 3.04 us -> 1.34 us
    convert_element_type x3 -> x0, other arithmetic: 2.73 us -> none  [the longest x1 1.4 us: in_kernel(): return (middle[:, None, :] + moe).astype(bf16)]
    concatenate x2 -> x0, local copies, waits for them, and re-layouts: 1.37 us -> none  [the longest x1 1.3 us: in_kernel(): jnp.concatenate([step_size[:, 0], decay_rate[None], skip_gain[None], writ...]
    reduce_sum x2 -> x0, other arithmetic: 0.85 us -> none  [the longest x1 0.76 us: in_kernel(): jnp.sum(jnp.where(expert_ids[:, 0, :, None] == jnp.arange(EXPERTS)[None,...]
    reshape x2 -> x0, local copies, waits for them, and re-layouts: 0.75 us -> none  [in_kernel(): lines = jnp.transpose(stream.astype(jnp.float32).reshape(STEPS, n, per, L...]
    concatenate x1 -> x0, other arithmetic: 0.69 us -> none  [in_kernel(): jnp.concatenate([lines, jnp.broadcast_to(gates[:, :, None], (n, STEPS, LA...]
    unnamed x1, local copies, waits for them, and re-layouts: 0.76 us -> 1.34 us
where the time goes in v3:
time: 38.4 us; the launch traced here: 38.1 us
  Pallas kernels  36.7 us (96%)
  local copies, waits for them, and re-layouts  1.34 us (3%)
    pallas_call x1, Pallas kernels, in_kernel(): pl.pallas_call(functools.partial(layer_kernel, n), out_shape=jax.ShapeDty...  36.7 us
    unnamed x1, local copies, waits for them, and re-layouts  1.34 us

profile of v3, /device:TPU:0, one launch (start us, length us, event | category | flops | bytes accessed | tf_op | source)
XLA Modules:
  0.0 38.1 jit_solution(14269558437488691062)
XLA Ops:
  0.0 36.7 %shard_map.145 = bf16[2,4096]{1,0:T(2,128)(2,1)} custom-call(f32[2,64]{1,0:T(2,128)} %bitcast.19, f32[1,64]{1,0:T(1,128)} %bitcast.21, f32[1,64]{1,0:T(1,128)} %bitcast.22, bf16[2,64]{1,0:T(2,128)(2,1)} %bitcast.23, bf16[2,64]{1,0:T(2,128)(2,1)} %bitcast.24, bf16[2,4096]{1,0:T(2,128)(2,1)} %bitcast.15, s32[2,2]{1,0:T(2,128)} %bitcast.20, ...), custom_call_target="tpu_custom_call" | custom-call | tf_op jit(solution)/shard_map/pallas_call | solution.py:363
  36.8 1.3 %copy.17 = bf16[2,1,4096]{2,0,1:T(2,128)(2,1)} copy(bf16[2,1,4096]{2,0,1:T(2,128)(2,1)} %bitcast.14) | data formatting | bytes 32768
